TPU v7x, 128 devices: a whole 4x4x4 slice. The times are simulated.
128 devices in a mesh: code: 4 (over y), row: 32 (over z, x, core).
Axes of the slice: x: 4, y: 4, z: 4, core: 2. Of those that a mesh axis runs over, the one named last changes fastest.
Arguments:
- residuals: bfloat16 [131072, 768], P(('code', 'row')), may hold values from -40 to 40
- codes: int32 [131072], P(('code', 'row')), may hold values from 0 to 7, as said below
- counts: int32 [4, 32, 4], P('code', 'row'), may hold values from 0 to 512, as said below
- centroids: float32 [8, 256, 768], P('code'), may hold values from -4 to 4
Outputs:
- centroids_out: float32 [8, 256, 768], P('code')
- residual_out: float32 [4, 32, 2048, 768], P('code', 'row')
Inputs may be any that keep to these rules, and one draw needn't show every extreme that they name: `counts`: each shard sends exactly 512 rows to one owner group and splits the rest among the others; all shards with index j = 0 along `row` send their 512 rows to the same owner group. `codes`: the rows of a shard are ordered by owner group code // 2, group 0 first, in blocks of the sizes given by counts.
All inputs are finite; a program needn't handle non-finite values.
Results may differ from a plain program's by a relative error of at most 0.0024.
Values may be sent and summed in bfloat16 or wider, within the bound.
A program may use at most 64 MiB of HBM per device.

v0:
```python
import jax
import jax.numpy as jnp
from jax import lax
from jax.sharding import PartitionSpec as P

ITERS = 3


score_scale = 0.0625


def per_device(residuals, codes, counts, centroids):
    width = residuals.shape[1]
    capacity = residuals.shape[0] // 2
    groups = lax.axis_size("code")
    per_group = centroids.shape[0]
    clusters = centroids.shape[1]
    sends = counts.reshape(groups)
    starts = jnp.cumsum(sends) - sends
    padded = jnp.concatenate([residuals, jnp.zeros((capacity, width), residuals.dtype)], 0)
    padcodes = jnp.concatenate([codes, jnp.zeros((capacity,), jnp.int32)], 0)
    slot = jnp.arange(capacity, dtype=jnp.int32)
    blocks = []
    labels = []
    for target in range(groups):
        piece = lax.dynamic_slice_in_dim(padded, starts[target], capacity, 0)
        tags = lax.dynamic_slice_in_dim(padcodes, starts[target], capacity, 0)
        live = slot < sends[target]
        blocks.append(jnp.where(live[:, None], piece, jnp.zeros_like(piece)))
        labels.append(jnp.where(live, tags - target * per_group, -1))
    arrived, tagged = (
        lax.all_to_all(jnp.stack(blocks), "code", split_axis=0, concat_axis=0, tiled=True),
        lax.all_to_all(jnp.stack(labels), "code", split_axis=0, concat_axis=0, tiled=True),
    )
    rows = arrived.reshape(groups * capacity, width)
    rows_wide = rows.astype(jnp.float32)
    tagged = tagged.reshape(groups * capacity)
    member = (tagged[:, None] == jnp.arange(per_group, dtype=jnp.int32)[None, :]).astype(
        jnp.float32
    )
    valid = jnp.sum(member, 1)
    cent = centroids
    weight = None
    for step in range(ITERS):
        flat = cent.reshape(per_group * clusters, width)
        cnorm = jnp.sum(flat * flat, 1).reshape(per_group, clusters)
        raw = jnp.dot(
            rows_wide, flat.T, precision=lax.Precision.HIGHEST, preferred_element_type=jnp.float32
        ).reshape(-1, per_group, clusters)
        scores = jnp.sum(member[:, :, None] * (score_scale * (2.0 * raw - cnorm[None])), 1)
        top = jnp.max(scores, 1, keepdims=True)
        expo = jnp.exp(scores - top)
        first = expo / jnp.sum(expo, 1, keepdims=True) * valid[:, None]
        colpart = jnp.sum(member[:, :, None] * first[:, None, :], 0)
        col = lax.psum(colpart, "row")
        colrow = jnp.sum(member[:, :, None] * col[None], 1) + (1.0 - valid)[:, None]
        quot = first / colrow
        prob = quot / (jnp.sum(quot, 1, keepdims=True) + (1.0 - valid)[:, None])
        weight = (member[:, :, None] * prob[:, None, :]).reshape(-1, per_group * clusters)
        num = jnp.dot(
            weight.T, rows_wide, precision=lax.Precision.HIGHEST, preferred_element_type=jnp.float32
        )
        mass = jnp.sum(weight, 0)
        total_num, total_mass = lax.psum((num, mass), "row")
        flat = total_num / total_mass[:, None]
        cent = flat.reshape(per_group, clusters, width)
    final = cent.reshape(per_group * clusters, width)
    recon = jnp.dot(
        weight, final, precision=lax.Precision.HIGHEST, preferred_element_type=jnp.float32
    )
    resid = rows_wide - recon
    return (cent, resid.reshape(1, 1, groups * capacity, width))


def solution(mesh):
    in_specs = (
        P(("code", "row"), None),
        P(("code", "row")),
        P("code", "row", None),
        P("code", None, None),
    )
    out_specs = (P("code", None, None), P("code", "row", None, None))
    return jax.shard_map(
        per_device, mesh=mesh, in_specs=in_specs, out_specs=out_specs, check_vma=False
    )
```

profile of v0, /device:TPU:1, one launch (start us, length us, event | category | flops | bytes accessed | tf_op | source)
XLA Modules:
  0.0 723.9 jit_solution(11863945113785906555)
XLA Ops:
  18.4 3.4 fusion.16
  22.5 5.0 all-to-all-start
  30.0 2.9 fusion.4
  32.9 1.9 pad_maximum_fusion
  34.8 4.3 all-to-all-start.1
  40.7 34.6 %all-to-all-done.1 = bf16[4,512,768]{2,1,0:T(8,128)(2,1)S(1)} async-done(((bf16[4,512,768]{2,1,0:T(8,128)(2,1)}), bf16[4,512,768]{2,1,0:T(8,128)(2,1)S(1)}, u32[]{:S(2)}, u32[]{:S(2)}) %all-to-all-start.1) | async-done | bytes 3145760 | tf_op jit(solution)/shard_map/all_to_all | solution.py:32
  75.3 1.7 copy-done.4
  77.0 7.6 %multiply_reduce_fusion.8 = f32[2048,256]{1,0:T(8,128)S(1)} fusion(bf16[2048,768,1]{1,0,2:T(8,128)(2,1)} %bitcast.61, f32[2,256,768]{2,1,0:T(8,128)} %param.7, f32[2048,2]{0,1:T(2,128)S(1)} %get-tuple-element.17, f32[2,256]{1,0:T(2,128)S(1)} %multiply_reduce_fusion.11), kind=kOutput, calls=%fused_computation.9 | convolution fusion | flops 9667346432 | bytes 6834176 | tf_op jit(solution)/shard_map/dot_general | solution.py:47
  85.6 2.0 divide_multiply_fusion.2
  87.6 2.9 copy.8
  90.5 2.0 multiply_reduce_fusion.7
  92.5 65.6 %psum.63 = f32[2,256]{1,0:T(2,128)S(1)} all-reduce(f32[2,256]{1,0:T(2,128)S(1)} %multiply_reduce_fusion.7), channel_id=1, replica_groups=mesh['code'=4,'row'=32] {'row'}, use_global_device_ids=true, to_apply=%region_7.8 | all-reduce | flops 512 | bytes 4096 | tf_op jit(solution)/shard_map/psum | solution.py:55
  159.8 2.9 copy.24
  162.7 2.9 divide_reduce_fusion.2
  165.7 3.1 multiply_divide_fusion.2
  168.7 1.9 copy.11
  172.6 6.6 fusion.29
  179.2 65.6 %psum.65 = f32[512]{0:T(512)S(1)} all-reduce(f32[512]{0:T(512)S(1)} %bitcast.76), channel_id=1, replica_groups=mesh['code'=4,'row'=32] {'row'}, use_global_device_ids=true, to_apply=%region_12.13 | all-reduce | flops 512 | bytes 4096 | tf_op jit(solution)/shard_map/psum | solution.py:64
  244.8 37.8 %all-reduce.6.cloned.1.call-done = f32[512,768]{1,0:T(8,128)} async-done(((f32[512,768]{1,0:T(8,128)}), f32[512,768]{1,0:T(8,128)}) %all-reduce.6.cloned.1.call-update) | async-done | bytes 1572880 | tf_op jit(solution)/shard_map/psum | solution.py:64
  282.6 2.8 multiply_reduce_fusion.10
  285.4 7.6 %multiply_reduce_fusion.5 = f32[2048,256]{1,0:T(8,128)S(1)} fusion(bf16[2048,768,1]{1,0,2:T(8,128)(2,1)} %bitcast.62, f32[2,256,768]{2,1,0:T(8,128)} %bitcast.69, f32[2,256]{1,0:T(2,128)S(1)} %sub.121, f32[2048,2]{0,1:T(2,128)S(1)} %get-tuple-element.17), kind=kOutput, calls=%fused_computation.6 | convolution fusion | flops 9667346432 | bytes 6834176 | tf_op jit(solution)/shard_map/dot_general | solution.py:47
  294.0 2.0 divide_multiply_fusion.1
  296.0 2.9 copy.13
  298.9 2.0 multiply_reduce_fusion.4
  300.9 62.9 %psum.66 = f32[2,256]{1,0:T(2,128)S(1)} all-reduce(f32[2,256]{1,0:T(2,128)S(1)} %multiply_reduce_fusion.4), channel_id=1, replica_groups=mesh['code'=4,'row'=32] {'row'}, use_global_device_ids=true, to_apply=%region_18.19 | all-reduce | flops 512 | bytes 4096 | tf_op jit(solution)/shard_map/psum | solution.py:55
  363.8 1.7 multiply_reduce_fusion.3
  365.4 2.9 copy.27
  368.3 2.9 divide_reduce_fusion.1
  371.3 3.1 multiply_divide_fusion.1
  374.4 1.9 copy.16
  378.2 6.6 fusion.30
  384.9 66.5 %psum.68 = f32[512]{0:T(512)S(1)} all-reduce(f32[512]{0:T(512)S(1)} %bitcast.77), channel_id=1, replica_groups=mesh['code'=4,'row'=32] {'row'}, use_global_device_ids=true, to_apply=%region_23.24 | all-reduce | flops 512 | bytes 4096 | tf_op jit(solution)/shard_map/psum | solution.py:64
  451.4 39.6 %all-reduce.8.cloned.1.call-done = f32[512,768]{1,0:T(8,128)} async-done(((f32[512,768]{1,0:T(8,128)}), f32[512,768]{1,0:T(8,128)}) %all-reduce.8.cloned.1.call-update) | async-done | bytes 1572880 | tf_op jit(solution)/shard_map/psum | solution.py:64
  491.0 2.8 multiply_reduce_fusion.9
  493.8 7.6 %multiply_reduce_fusion.2 = f32[2048,256]{1,0:T(8,128)S(1)} fusion(bf16[2048,768,1]{1,0,2:T(8,128)(2,1)} %bitcast.63, f32[2,256,768]{2,1,0:T(8,128)} %bitcast.68, f32[2,256]{1,0:T(2,128)S(1)} %sub.126, f32[2048,2]{0,1:T(2,128)S(1)} %get-tuple-element.17), kind=kOutput, calls=%fused_computation.3 | convolution fusion | flops 9667346432 | bytes 6834176 | tf_op jit(solution)/shard_map/dot_general | solution.py:47
  502.4 2.0 divide_multiply_fusion
  504.4 2.9 copy.18
  507.3 2.0 multiply_reduce_fusion.1
  509.3 63.2 %psum.69 = f32[2,256]{1,0:T(2,128)S(1)} all-reduce(f32[2,256]{1,0:T(2,128)S(1)} %multiply_reduce_fusion.1), channel_id=1, replica_groups=mesh['code'=4,'row'=32] {'row'}, use_global_device_ids=true, to_apply=%region_29.30 | all-reduce | flops 512 | bytes 4096 | tf_op jit(solution)/shard_map/psum | solution.py:55
  574.1 2.9 copy.30
  577.0 2.9 divide_reduce_fusion
  580.0 3.1 multiply_divide_fusion
  583.1 1.9 copy.21
  585.4 2.0 copy-done.3
  588.1 6.6 fusion.31
  594.7 66.7 %psum.71 = f32[512]{0:T(512)S(1)} all-reduce(f32[512]{0:T(512)S(1)} %bitcast.78), channel_id=1, replica_groups=mesh['code'=4,'row'=32] {'row'}, use_global_device_ids=true, to_apply=%region_34.35 | all-reduce | flops 512 | bytes 4096 | tf_op jit(solution)/shard_map/psum | solution.py:64
  661.4 39.4 %all-reduce.10.cloned.1.call-done = f32[512,768]{1,0:T(8,128)} async-done(((f32[512,768]{1,0:T(8,128)}), f32[512,768]{1,0:T(8,128)}) %all-reduce.10.cloned.1.call-update) | async-done | bytes 1572880 | tf_op jit(solution)/shard_map/psum | solution.py:64
  702.4 14.7 %subtract_bitcast_fusion = f32[1,1,2048,768]{3,2,1,0:T(8,128)} fusion(bf16[2048,768]{1,0:T(8,128)(2,1)S(1)} %bitcast.67, f32[2048,512]{0,1:T(8,128)} %bitcast.58, f32[512,768]{1,0:T(8,128)S(1)} %broadcast_divide_fusion), kind=kOutput, calls=%fused_computation | convolution fusion | flops 9666822144 | bytes 15204352 | tf_op jit(solution)/shard_map/dot_general | solution.py:68
  (57 shorter events, 21.2 us)
Async XLA Ops:
  22.5 12.3 %all-to-all-start = ((s32[4,1,512]{2,1,0:T(1,128)}), s32[4,1,512]{2,1,0:T(1,128)S(1)}, u32[]{:S(2)}, u32[]{:S(2)}) async-start(s32[4,1,512]{2,1,0:T(1,128)} %all_to_all.9), calls=%async_computation | async-start | bytes 16384 | tf_op jit(solution)/shard_map/all_to_all | solution.py:33
  34.8 40.6 %all-to-all-start.1 = ((bf16[4,512,768]{2,1,0:T(8,128)(2,1)}), bf16[4,512,768]{2,1,0:T(8,128)(2,1)S(1)}, u32[]{:S(2)}, u32[]{:S(2)}) async-start(bf16[4,512,768]{2,1,0:T(8,128)(2,1)} %pad_maximum_fusion), calls=%async_computation.1 | async-start | bytes 6291456 | tf_op jit(solution)/shard_map/all_to_all | solution.py:32
  39.1 243.5 %all-reduce.6.cloned.1.call-start = ((), (), s32[]{:S(2)}) async-start(), calls=%async_computation.2 | async-start | bytes 3145728 | tf_op jit(solution)/shard_map/psum | solution.py:64
  75.3 1.7 copy-start.4
  162.7 3.0 copy-start.1
  170.7 1.9 copy-start.5
  179.2 311.8 %all-reduce.8.cloned.1.call-start = ((), (), s32[]{:S(2)}) async-start(), calls=%async_computation.3 | async-start | bytes 3145728 | tf_op jit(solution)/shard_map/psum | solution.py:64
  368.3 3.0 copy-start.2
  376.3 1.9 copy-start.6
  384.8 316.0 %all-reduce.10.cloned.1.call-start = ((), (), s32[]{:S(2)}) async-start(), calls=%async_computation.4 | async-start | bytes 3145728 | tf_op jit(solution)/shard_map/psum | solution.py:64
  577.0 3.0 copy-start
  585.0 3.1 copy-start.7
  585.4 2.0 copy-start.3
  594.6 107.7 %copy-start.8 = (bf16[4,512,768]{2,1,0:T(8,128)(2,1)S(1)}, bf16[4,512,768]{2,1,0:T(8,128)(2,1)}, u32[]{:S(2)}) copy-start(bf16[4,512,768]{2,1,0:T(8,128)(2,1)} %copy-done.4) | copy-start | bytes 9437188
  702.4 14.7 %copy-start.9 = (f32[512,768]{1,0:T(8,128)}, f32[512,768]{1,0:T(8,128)S(1)}, u32[]{:S(2)}) copy-start(f32[512,768]{1,0:T(8,128)S(1)} %broadcast_divide_fusion) | copy-start | bytes 4718596
Sparse Core Ops, SparseCore 0:
  179.3 103.2 all-reduce.5
  384.9 106.0 all-reduce.7
  594.8 105.9 all-reduce.9
where the time goes:
time: 730 us; the launch traced here: 724 us
  blocking collectives  391 us (54%)
  waiting for transfers between devices  151 us (21%)
  other arithmetic  60.3 us (8%)
  matrix products  57.2 us (8%)
  local copies, waits for them, and re-layouts  33.1 us (5%)
  between operations  21.9 us (3%)
  starting transfers between devices  9.42 us (1%)
    psum x3, blocking collectives, per_device(): total_num, total_mass = lax.psum((num, mass), 'row')  199 us
    psum x3, blocking collectives, per_device(): col = lax.psum(colpart, 'row')  192 us
    psum x3, waiting for transfers between devices, per_device(): total_num, total_mass = lax.psum((num, mass), 'row')  117 us
    all_to_all x1, waiting for transfers between devices, per_device(): lax.all_to_all(jnp.stack(blocks), 'code', split_axis=0, concat_axis=0, ti...  34.6 us
    dot_general x3, matrix products, per_device(): jnp.dot(rows_wide, flat.T, precision=lax.Precision.HIGHEST, preferred_ele...  22.8 us
    dot_general x3, matrix products, per_device(): jnp.dot(weight.T, rows_wide, precision=lax.Precision.HIGHEST, preferred_e...  19.7 us
    unnamed x26, local copies, waits for them, and re-layouts  15.9 us
    dot_general x1, matrix products, per_device(): jnp.dot(weight, final, precision=lax.Precision.HIGHEST, preferred_element...  14.7 us
  transfers between devices with their start and end apart: 5, of which 4 were waited for; matrix products, arithmetic and copies ran while one was open for 1% of the time, Pallas kernels for 0%

commit v1 on v0

v1 whole, which is shorter than its diff:
```python
import jax
import jax.numpy as jnp
from jax import lax
from jax.experimental import pallas as pl
from jax.experimental.pallas import tpu as pltpu
from jax.sharding import PartitionSpec as P

ITERS = 3
SCORE_SCALE = 0.0625
LOG2E = 1.4426950408889634
MESH = pl.DeviceIdType.MESH
GROUPS = 4
CHIPS = 16
SIDE = 4
LANES = 128
CAP = 512
CHUNK = 128
F32 = jnp.float32
BF16 = jnp.bfloat16

NT = (((1,), (1,)), ((), ()))
TN = (((0,), (0,)), ((), ()))


def wait_bytes(ref, sem):
    pltpu.make_async_copy(ref, ref, sem).wait()


def kernel(
    x_hbm, codes_ref, counts_ref, cent_hbm, cout_ref, rout_ref,
    x_ref, cent_ref, sendbuf, sendtag, rows, tags, p0, phi, plo, colsend, colrecv, numsend, numrecv,
    massacc, massrecv, call, chi, clo, cn, colacc, pother, cother, res,
    in_sem, asend, tsend, arecv, trecv, fsend, ftsend, frecv, ftrecv,
    col_s, col_r, rs_s, rs_r, m_s, m_r, ag_s, ag_r, po_s, po_r, co_s, co_r, out_sem,
):
    i = lax.axis_index("code")
    j = lax.axis_index("row")
    core = lax.rem(j, 2)
    chip = lax.div(j, 2)
    cz = lax.div(chip, SIDE)
    cx = lax.rem(chip, SIDE)
    sib = (i, 2 * chip + 1 - core)
    share = numrecv.shape[1]
    clusters = call.shape[0]
    width = call.shape[1]

    def chip_at(d):
        return lax.rem(cz + lax.div(d, SIDE), SIDE) * SIDE + lax.rem(cx + lax.rem(d, SIDE), SIDE)

    def row_peer(t):
        return (i, 2 * t + core)

    def group(d):
        return lax.rem(i + d, GROUPS)

    load_x = pltpu.make_async_copy(x_hbm, x_ref, in_sem.at[0])
    load_x.start()
    load_c = pltpu.make_async_copy(cent_hbm.at[core], cent_ref, in_sem.at[1])
    load_c.start()

    barrier = pltpu.get_barrier_semaphore()
    for d in range(1, GROUPS):
        pl.semaphore_signal(barrier, inc=1, device_id=(group(d), j), device_id_type=MESH)
    pl.semaphore_signal(barrier, inc=1, device_id=sib, device_id_type=MESH)

    def greet(d, carry):
        pl.semaphore_signal(barrier, inc=1, device_id=row_peer(chip_at(d)), device_id_type=MESH)
        return carry

    lax.fori_loop(1, CHIPS, greet, 0)

    load_x.wait()
    half = CAP // 2
    iota_r = lax.broadcasted_iota(jnp.int32, (half, x_ref.shape[0]), 1)
    iota_t = lax.broadcasted_iota(jnp.int32, (half, x_ref.shape[0]), 0)
    diff = iota_r - iota_t
    codes8 = jnp.broadcast_to(codes_ref[...], (8, codes_ref.shape[1]))

    def block(d, h):
        target = group(d)
        start = jnp.int32(0)
        for g in range(GROUPS - 1):
            start = start + jnp.where(g < target, counts_ref[g], 0)
        number = counts_ref[target] - h * half
        pick = jnp.where((diff == start + h * half) & (iota_t < number), 1.0, 0.0).astype(BF16)
        piece = jnp.dot(pick, x_ref[...], preferred_element_type=F32).astype(BF16)
        label = (codes8 - 2 * target + 1).astype(F32).astype(BF16)
        tag = lax.dot_general(label, pick, NT, preferred_element_type=F32)
        return piece, tag

    def a2a_copy(d, q):
        lines = pl.ds(q * CHUNK, CHUNK)
        return pltpu.make_async_remote_copy(
            sendbuf.at[d - 1, lines], rows.at[core * GROUPS + d, lines], asend, arecv.at[d - 1, q],
            device_id=(group(d), j), device_id_type=MESH,
        )

    def tag_copy(d):
        return pltpu.make_async_remote_copy(
            sendtag.at[d - 1], tags.at[core * GROUPS + d], tsend, trecv.at[d - 1],
            device_id=(group(d), j), device_id_type=MESH,
        )

    def forward_copy(d, q):
        lines = pl.ds(q * CHUNK, CHUNK)
        return pltpu.make_async_remote_copy(
            rows.at[core * GROUPS + d, lines], rows.at[core * GROUPS + d, lines], fsend, frecv.at[d, q],
            device_id=sib, device_id_type=MESH,
        )

    def forward_tag(d):
        return pltpu.make_async_remote_copy(
            tags.at[core * GROUPS + d], tags.at[core * GROUPS + d], ftsend, ftrecv.at[d],
            device_id=sib, device_id_type=MESH,
        )

    quarters = CAP // CHUNK
    first = True
    for h in range(2):
        for d in (2, 1, 3):
            piece, tag = block(d, h)
            sendbuf[d - 1, h * half : (h + 1) * half, :] = piece
            sendtag[d - 1, :, h * half : (h + 1) * half] = tag
            if first:
                pl.semaphore_wait(barrier, GROUPS - 1 + 1 + CHIPS - 1)
                first = False
            if h == 1:
                tag_copy(d).start()
            for q in range(quarters // 2):
                a2a_copy(d, h * (quarters // 2) + q).start()
    for h in range(2):
        piece, tag = block(0, h)
        rows[core * GROUPS, h * half : (h + 1) * half, :] = piece
        tags[core * GROUPS, :, h * half : (h + 1) * half] = tag
    forward_tag(0).start()

    def own_forward(q, carry):
        forward_copy(0, q).start()
        return carry

    lax.fori_loop(0, quarters, own_forward, 0)

    def split(c):
        hi = c.astype(BF16)
        chi[...] = hi
        clo[...] = (c - hi.astype(F32)).astype(BF16)
        norm = jnp.sum(c * c, axis=1, keepdims=True) * (SCORE_SCALE * LOG2E)
        cn[...] = jnp.broadcast_to(norm, cn.shape)

    def first_soft(b, lo, n):
        x = rows[b, pl.ds(lo, n), :]
        s = lax.dot_general(chi[...], x, NT, preferred_element_type=F32)
        s = s + lax.dot_general(clo[...], x, NT, preferred_element_type=F32)
        for k in range(n // LANES):
            at = pl.ds(lo + k * LANES, LANES)
            t = s[:, k * LANES : (k + 1) * LANES] * (2.0 * SCORE_SCALE * LOG2E) - cn[...]
            e = jnp.exp2(t - jnp.max(t, axis=0, keepdims=True))
            total = jnp.sum(e, axis=0, keepdims=True)
            live = tags[b, 0:1, at] == (core + 1).astype(F32)
            p = e * jnp.where(live, 1.0 / total, 0.0)
            p0[b, :, at] = p
            colacc[...] += p

    load_c.wait()
    split(cent_ref[...])
    colacc[...] = jnp.zeros_like(colacc)

    other = 1 - core

    def own_soft(q, carry):
        lo = pl.multiple_of(q * CHUNK, CHUNK)
        first_soft(core * GROUPS, lo, CHUNK)
        return carry

    lax.fori_loop(0, quarters, own_soft, 0)
    forward_tag(0).wait_recv()

    def sib_soft(q, carry):
        lo = pl.multiple_of(q * CHUNK, CHUNK)
        forward_copy(0, q).wait_recv()
        first_soft(other * GROUPS, lo, CHUNK)
        return carry

    lax.fori_loop(0, quarters, sib_soft, 0)

    for d in (2, 1, 3):
        tag_copy(d).wait_recv()
        forward_tag(d).start()

    def sib_tag(d, carry):
        forward_tag(d).wait_recv()
        return carry

    lax.fori_loop(1, GROUPS, sib_tag, 0)

    def arrive(t, carry):
        q = lax.div(t, GROUPS - 1)
        d = lax.rem(t, GROUPS - 1) + 1
        lo = pl.multiple_of(q * CHUNK, CHUNK)
        a2a_copy(d, q).wait_recv()
        forward_copy(d, q).start()
        first_soft(core * GROUPS + d, lo, CHUNK)
        forward_copy(d, q).wait_recv()
        first_soft(other * GROUPS + d, lo, CHUNK)
        return carry

    lax.fori_loop(0, quarters * (GROUPS - 1), arrive, 0)

    def chunk_of(t):
        return pl.ds(pl.multiple_of(t * share, share), share)

    mine = chunk_of(chip)

    def col_copy(d):
        return pltpu.make_async_remote_copy(
            colsend, colrecv.at[d - 1], col_s, col_r, device_id=row_peer(chip_at(d)), device_id_type=MESH
        )

    def rs_copy(d):
        t = chip_at(d)
        return pltpu.make_async_remote_copy(
            numsend.at[chunk_of(t)], numrecv.at[d - 1], rs_s, rs_r, device_id=row_peer(t), device_id_type=MESH
        )

    def mass_copy(d):
        t = chip_at(d)
        return pltpu.make_async_remote_copy(
            massacc.at[chunk_of(t)], massrecv.at[d - 1], m_s, m_r, device_id=row_peer(t), device_id_type=MESH
        )

    def ag_copy(d):
        return pltpu.make_async_remote_copy(
            call.at[mine], call.at[mine], ag_s, ag_r, device_id=row_peer(chip_at(d)), device_id_type=MESH
        )

    def each_peer(make):
        def body(d, carry):
            make(d).start()
            return carry

        lax.fori_loop(1, CHIPS, body, 0)

    blocks = 2 * GROUPS
    rest = pl.ds(0, (CHIPS - 1) * share)

    def update(step, carry):
        acc = jnp.transpose(colacc[...])
        colsend[...] = jnp.sum(acc.reshape(LANES // 8, 8, clusters), axis=0)
        each_peer(col_copy)
        massacc[...] = jnp.zeros_like(massacc)
        wait_bytes(colrecv, col_r)
        col = colsend[...] + jnp.sum(colrecv[...], axis=0)
        inverse = 1.0 / jnp.sum(col, axis=0, keepdims=True)
        icol = jnp.transpose(jnp.broadcast_to(inverse, (LANES, clusters)))
        colacc[...] = icol

        def weigh(b, carry):
            for k in range(CAP // LANES):
                at = slice(k * LANES, (k + 1) * LANES)
                q = p0[b, :, at] * colacc[...]
                total = jnp.sum(q, axis=0, keepdims=True)
                live = tags[b, 0:1, at] == (core + 1).astype(F32)
                p = q * jnp.where(live, 1.0 / jnp.where(live, total, 1.0), 0.0)
                hi = p.astype(BF16)
                phi[b, :, at] = hi
                plo[b, :, at] = (p - hi.astype(F32)).astype(BF16)
                massacc[...] += p
            x = rows[b]
            part = jnp.dot(phi[b], x, preferred_element_type=F32)
            part = part + jnp.dot(plo[b], x, preferred_element_type=F32)

            @pl.when(b == 0)
            def _():
                numsend[...] = part

            @pl.when(b > 0)
            def _():
                numsend[...] += part

            return carry

        lax.fori_loop(0, blocks, weigh, 0)
        each_peer(rs_copy)
        each_peer(mass_copy)
        wait_bytes(colrecv, col_s)
        wait_bytes(massrecv, m_r)
        wait_bytes(numrecv, rs_r)
        mass = massacc[mine, :] + jnp.sum(massrecv[...], axis=0)
        num = numsend[mine, :] + jnp.sum(numrecv[...], axis=0)
        call[mine, :] = num / jnp.sum(mass, axis=1, keepdims=True)
        each_peer(ag_copy)
        wait_bytes(massrecv, m_s)
        wait_bytes(numrecv, rs_s)
        wait_bytes(call.at[rest], ag_r)
        wait_bytes(call.at[rest], ag_s)
        split(call[...])

        @pl.when(step < ITERS - 1)
        def _():
            colacc[...] = jnp.zeros_like(colacc)

            def soft(b, carry):
                first_soft(b, 0, CAP)
                return carry

            lax.fori_loop(0, blocks, soft, 0)

        return carry

    lax.fori_loop(0, ITERS, update, 0)

    pcopy = pltpu.make_async_remote_copy(
        phi.at[pl.ds(other * GROUPS, GROUPS)], pother, po_s, po_r, device_id=sib, device_id_type=MESH
    )
    pcopy.start()
    ccopy = pltpu.make_async_remote_copy(call, cother, co_s, co_r, device_id=sib, device_id_type=MESH)
    ccopy.start()
    own_out = pltpu.make_async_copy(call, cout_ref.at[core], in_sem.at[0])
    own_out.start()
    wait_bytes(sendbuf, asend)
    wait_bytes(sendtag, tsend)
    wait_bytes(rows.at[pl.ds(0, GROUPS)], fsend)
    wait_bytes(tags.at[pl.ds(0, GROUPS)], ftsend)
    pcopy.wait()
    ccopy.wait()
    other_out = pltpu.make_async_copy(cother, cout_ref.at[other], in_sem.at[1])
    other_out.start()
    ohi = cother[...].astype(BF16)
    olo = (cother[...] - ohi.astype(F32)).astype(BF16)
    x_ref[0:clusters, :] = ohi
    x_ref[clusters : 2 * clusters, :] = olo

    def out_copy(d):
        return pltpu.make_async_copy(res.at[d], rout_ref.at[lax.rem(i + GROUPS - d, GROUPS)], out_sem.at[d])

    def finish(d, carry):
        p = phi[core * GROUPS + d]
        recon = lax.dot_general(p, chi[...], TN, preferred_element_type=F32)
        recon = recon + lax.dot_general(p, clo[...], TN, preferred_element_type=F32)
        p = pother[d]
        recon = recon + lax.dot_general(p, x_ref[0:clusters, :], TN, preferred_element_type=F32)
        recon = recon + lax.dot_general(p, x_ref[clusters : 2 * clusters, :], TN, preferred_element_type=F32)
        res[d] = rows[core * GROUPS + d].astype(F32) - recon
        out_copy(d).start()
        return carry

    lax.fori_loop(0, GROUPS, finish, 0)
    own_out.wait()
    other_out.wait()

    def drain(d, carry):
        out_copy(d).wait()
        return carry

    lax.fori_loop(0, GROUPS, drain, 0)


def per_device(residuals, codes, counts, centroids):
    nrow, width = residuals.shape
    clusters = centroids.shape[1]
    share = clusters // CHIPS
    blocks = 2 * GROUPS
    dma = pltpu.SemaphoreType.DMA
    quarters = CAP // CHUNK
    scratch = [
        pltpu.VMEM((nrow, width), BF16),
        pltpu.VMEM((clusters, width), F32),
        pltpu.VMEM((GROUPS - 1, CAP, width), BF16),
        pltpu.VMEM((GROUPS - 1, 8, CAP), F32),
        pltpu.VMEM((blocks, CAP, width), BF16),
        pltpu.VMEM((blocks, 8, CAP), F32),
        pltpu.VMEM((blocks, clusters, CAP), F32),
        pltpu.VMEM((blocks, clusters, CAP), BF16),
        pltpu.VMEM((blocks, clusters, CAP), BF16),
        pltpu.VMEM((8, clusters), F32),
        pltpu.VMEM((CHIPS - 1, 8, clusters), F32),
        pltpu.VMEM((clusters, width), F32),
        pltpu.VMEM((CHIPS - 1, share, width), F32),
        pltpu.VMEM((clusters, LANES), F32),
        pltpu.VMEM((CHIPS - 1, share, LANES), F32),
        pltpu.VMEM((clusters, width), F32),
        pltpu.VMEM((clusters, width), BF16),
        pltpu.VMEM((clusters, width), BF16),
        pltpu.VMEM((clusters, LANES), F32),
        pltpu.VMEM((clusters, LANES), F32),
        pltpu.VMEM((GROUPS, clusters, CAP), BF16),
        pltpu.VMEM((clusters, width), F32),
        pltpu.VMEM((GROUPS, CAP, width), F32),
        dma((2,)),
        dma, dma, dma((GROUPS - 1, quarters)), dma((GROUPS - 1,)),
        dma, dma, dma((GROUPS, quarters)), dma((GROUPS,)),
        dma, dma, dma, dma, dma, dma, dma, dma,
        dma, dma, dma, dma, dma((GROUPS,)),
    ]
    cent, resid = pl.pallas_call(
        kernel,
        out_shape=(
            jax.ShapeDtypeStruct(centroids.shape, F32),
            jax.ShapeDtypeStruct((GROUPS, CAP, width), F32),
        ),
        in_specs=[
            pl.BlockSpec(memory_space=pl.ANY),
            pl.BlockSpec(memory_space=pltpu.VMEM),
            pl.BlockSpec(memory_space=pltpu.SMEM),
            pl.BlockSpec(memory_space=pl.ANY),
        ],
        out_specs=(pl.BlockSpec(memory_space=pl.ANY), pl.BlockSpec(memory_space=pl.ANY)),
        scratch_shapes=scratch,
        compiler_params=pltpu.CompilerParams(
            collective_id=0, has_side_effects=True, vmem_limit_bytes=56 * 1024 * 1024
        ),
    )(residuals, codes.reshape(1, nrow), counts.reshape(GROUPS), centroids)
    return cent, resid.reshape(1, 1, GROUPS * CAP, width)


def solution(mesh):
    in_specs = (
        P(("code", "row"), None),
        P(("code", "row")),
        P("code", "row", None),
        P("code", None, None),
    )
    out_specs = (P("code", None, None), P("code", "row", None, None))
    return jax.shard_map(
        per_device, mesh=mesh, in_specs=in_specs, out_specs=out_specs, check_vma=False
    )
```

time: 730 us -> 196 us (0.27)
  blocking collectives: 391 us -> 0 us
  Pallas kernels: 0 us -> 186 us
  waiting for transfers between devices: 151 us -> 0 us
  other arithmetic: 60.3 us -> 0 us
  matrix products: 57.2 us -> 0 us
  local copies, waits for them, and re-layouts: 33.1 us -> 8.54 us
  between operations: 21.9 us -> 0.64 us
  starting transfers between devices: 9.42 us -> 0 us
    psum x6 -> x0, blocking collectives: 391 us -> none  [the longest x3 199 us: per_device(): total_num, total_mass = lax.psum((num, mass), 'row')]
    pallas_call x0 -> x1, Pallas kernels: none -> 186 us  [per_device(): pl.pallas_call(kernel, out_shape=(jax.ShapeDtypeStruct(centroids.shape, F...]
    psum x3 -> x0, waiting for transfers between devices: 117 us -> none  [per_device(): total_num, total_mass = lax.psum((num, mass), 'row')]
    dot_general x7 -> x0, matrix products: 57.2 us -> none  [the longest x3 22.8 us: per_device(): jnp.dot(rows_wide, flat.T, precision=lax.Precision.HIGHEST, preferred_ele...]
    all_to_all x2 -> x0, waiting for transfers between devices: 34.6 us -> none  [the longest x1 34.6 us: per_device(): lax.all_to_all(jnp.stack(blocks), 'code', split_axis=0, concat_axis=0, ti...]
    reduce_sum x19 -> x0, other arithmetic: 30.2 us -> none  [the longest x3 8.85 us: per_device(): prob = quot / (jnp.sum(quot, 1, keepdims=True) + (1.0 - valid)[:, None])]
    div x4 -> x0, other arithmetic: 10.8 us -> none  [the longest x3 9.23 us: per_device(): prob = quot / (jnp.sum(quot, 1, keepdims=True) + (1.0 - valid)[:, None])]
    all_to_all x2 -> x0, starting transfers between devices: 9.34 us -> none  [the longest x1 5.01 us: per_device(): lax.all_to_all(jnp.stack(labels), 'code', split_axis=0, concat_axis=0, ti...]
  transfers between devices with their start and end apart: 5 -> 0, of which waited for: 4 -> 0; matrix products, arithmetic and copies ran while one was open for 1% -> 0% of each run, Pallas kernels for 0% -> 0%
where the time goes in v1:
time: 196 us; the launch traced here: 195 us
  Pallas kernels  186 us (95%)
  local copies, waits for them, and re-layouts  8.54 us (4%)
    pallas_call x1, Pallas kernels, per_device(): pl.pallas_call(kernel, out_shape=(jax.ShapeDtypeStruct(centroids.shape, F...  186 us
    unnamed x2, local copies, waits for them, and re-layouts  8.54 us

profile of v1, /device:TPU:1, one launch (start us, length us, event | category | flops | bytes accessed | tf_op | source)
XLA Modules:
  0.0 195.3 jit_solution(14362209153098678185)
XLA Ops:
  0.6 186.1 %shard_map.59 = (f32[2,256,768]{2,1,0:T(8,128)}, f32[4,512,768]{2,1,0:T(8,128)}) custom-call(bf16[1024,768]{1,0:T(8,128)(2,1)} %x_hbm.1, s32[1,1024]{1,0:T(1,128)} %bitcast.4, s32[4]{0:T(128)} %bitcast.5, f32[2,256,768]{2,1,0:T(8,128)} %cent_hbm.1), custom_call_target="tpu_custom_call" | custom-call | tf_op jit(solution)/shard_map/pallas_call | solution.py:395
  186.7 2.7 %copy.8 = f32[2,256,768]{2,1,0:T(8,128)} copy(f32[2,256,768]{2,1,0:T(8,128)} %get-tuple-element.8) | data formatting | bytes 3145728
  189.4 5.9 %copy.9 = f32[1,1,2048,768]{3,2,1,0:T(8,128)} copy(f32[1,1,2048,768]{3,2,1,0:T(8,128)} %bitcast.3) | data formatting | bytes 12582912

commit v2 on v1

--- a/solution.py
+++ b/solution.py
@@ -27,11 +27,11 @@
 
 
 def kernel(
-    x_hbm, codes_ref, counts_ref, cent_hbm, cout_ref, rout_ref,
-    x_ref, cent_ref, sendbuf, sendtag, rows, tags, p0, phi, plo, colsend, colrecv, numsend, numrecv,
-    massacc, massrecv, call, chi, clo, cn, colacc, pother, cother, res,
+    x_hbm, codes_ref, counts_ref, cent_hbm, cent_out, rows_out, p_out,
+    x_ref, cent_ref, sendbuf, sendtag, rows, tags, p0, p2, colsend, colrecv, numsend, numrecv,
+    masssend, massrecv, call, c2, cn, colacc, massacc,
     in_sem, asend, tsend, arecv, trecv, fsend, ftsend, frecv, ftrecv,
-    col_s, col_r, rs_s, rs_r, m_s, m_r, ag_s, ag_r, po_s, po_r, co_s, co_r, out_sem,
+    col_s, col_r, rs_s, rs_r, m_s, m_r, ag_s, ag_r, po_s, po_r, co_s, co_r, rows_sem, p_sem,
 ):
     i = lax.axis_index("code")
     j = lax.axis_index("row")
@@ -52,6 +52,9 @@
 
     def group(d):
         return lax.rem(i + d, GROUPS)
+
+    def source(d):
+        return lax.rem(i + GROUPS - d, GROUPS)
 
     load_x = pltpu.make_async_copy(x_hbm, x_ref, in_sem.at[0])
     load_x.start()
@@ -142,15 +145,15 @@
 
     def split(c):
         hi = c.astype(BF16)
-        chi[...] = hi
-        clo[...] = (c - hi.astype(F32)).astype(BF16)
+        c2[0:clusters, :] = hi
+        c2[clusters : 2 * clusters, :] = (c - hi.astype(F32)).astype(BF16)
         norm = jnp.sum(c * c, axis=1, keepdims=True) * (SCORE_SCALE * LOG2E)
         cn[...] = jnp.broadcast_to(norm, cn.shape)
 
     def first_soft(b, lo, n):
         x = rows[b, pl.ds(lo, n), :]
-        s = lax.dot_general(chi[...], x, NT, preferred_element_type=F32)
-        s = s + lax.dot_general(clo[...], x, NT, preferred_element_type=F32)
+        s = lax.dot_general(c2[...], x, NT, preferred_element_type=F32)
+        s = s[0:clusters] + s[clusters : 2 * clusters]
         for k in range(n // LANES):
             at = pl.ds(lo + k * LANES, LANES)
             t = s[:, k * LANES : (k + 1) * LANES] * (2.0 * SCORE_SCALE * LOG2E) - cn[...]
@@ -167,22 +170,6 @@
 
     other = 1 - core
 
-    def own_soft(q, carry):
-        lo = pl.multiple_of(q * CHUNK, CHUNK)
-        first_soft(core * GROUPS, lo, CHUNK)
-        return carry
-
-    lax.fori_loop(0, quarters, own_soft, 0)
-    forward_tag(0).wait_recv()
-
-    def sib_soft(q, carry):
-        lo = pl.multiple_of(q * CHUNK, CHUNK)
-        forward_copy(0, q).wait_recv()
-        first_soft(other * GROUPS, lo, CHUNK)
-        return carry
-
-    lax.fori_loop(0, quarters, sib_soft, 0)
-
     for d in (2, 1, 3):
         tag_copy(d).wait_recv()
         forward_tag(d).start()
@@ -191,20 +178,57 @@
         forward_tag(d).wait_recv()
         return carry
 
-    lax.fori_loop(1, GROUPS, sib_tag, 0)
+    lax.fori_loop(0, GROUPS, sib_tag, 0)
+
+    def sib_soft(d, q):
+        forward_copy(d, q).wait_recv()
+        first_soft(other * GROUPS + d, pl.multiple_of(q * CHUNK, CHUNK), CHUNK)
+
+    def own_soft(q, carry):
+        first_soft(core * GROUPS, pl.multiple_of(q * CHUNK, CHUNK), CHUNK)
+        sib_soft(0, q)
+        return carry
+
+    lax.fori_loop(0, quarters, own_soft, 0)
+
+    def place(t):
+        return lax.rem(t, GROUPS - 1) + 1, lax.div(t, GROUPS - 1)
 
     def arrive(t, carry):
-        q = lax.div(t, GROUPS - 1)
-        d = lax.rem(t, GROUPS - 1) + 1
-        lo = pl.multiple_of(q * CHUNK, CHUNK)
+        d, q = place(t)
         a2a_copy(d, q).wait_recv()
         forward_copy(d, q).start()
-        first_soft(core * GROUPS + d, lo, CHUNK)
-        forward_copy(d, q).wait_recv()
-        first_soft(other * GROUPS + d, lo, CHUNK)
-        return carry
-
-    lax.fori_loop(0, quarters * (GROUPS - 1), arrive, 0)
+        first_soft(core * GROUPS + d, pl.multiple_of(q * CHUNK, CHUNK), CHUNK)
+
+        @pl.when(t > 0)
+        def _():
+            sib_soft(*place(t - 1))
+
+        return carry
+
+    arrivals = quarters * (GROUPS - 1)
+    lax.fori_loop(0, arrivals, arrive, 0)
+
+    def rows_copy(d):
+        return pltpu.make_async_copy(rows.at[core * GROUPS + d], rows_out.at[source(d)], rows_sem.at[d])
+
+    def p_copy(d):
+        return pltpu.make_async_copy(
+            p2.at[core * GROUPS + d, pl.ds(0, clusters)], p_out.at[source(d), core], p_sem.at[d]
+        )
+
+    def p_forward(d):
+        return pltpu.make_async_remote_copy(
+            p2.at[other * GROUPS + d, pl.ds(0, clusters)], p_out.at[source(d), core], po_s.at[d], po_r.at[d],
+            device_id=sib, device_id_type=MESH,
+        )
+
+    def rows_start(d, carry):
+        rows_copy(d).start()
+        return carry
+
+    lax.fori_loop(0, GROUPS, rows_start, 0)
+    sib_soft(GROUPS - 1, quarters - 1)
 
     def chunk_of(t):
         return pl.ds(pl.multiple_of(t * share, share), share)
@@ -223,9 +247,8 @@
         )
 
     def mass_copy(d):
-        t = chip_at(d)
-        return pltpu.make_async_remote_copy(
-            massacc.at[chunk_of(t)], massrecv.at[d - 1], m_s, m_r, device_id=row_peer(t), device_id_type=MESH
+        return pltpu.make_async_remote_copy(
+            masssend, massrecv.at[d - 1], m_s, m_r, device_id=row_peer(chip_at(d)), device_id_type=MESH
         )
 
     def ag_copy(d):
@@ -243,16 +266,18 @@
     blocks = 2 * GROUPS
     rest = pl.ds(0, (CHIPS - 1) * share)
 
+    def as_row(parts):
+        return jnp.sum(jnp.transpose(parts), axis=0, keepdims=True)
+
+    def as_column(row):
+        return jnp.transpose(jnp.broadcast_to(row, (LANES, clusters)))
+
     def update(step, carry):
-        acc = jnp.transpose(colacc[...])
-        colsend[...] = jnp.sum(acc.reshape(LANES // 8, 8, clusters), axis=0)
+        colsend[...] = as_row(colacc[...])
         each_peer(col_copy)
         massacc[...] = jnp.zeros_like(massacc)
         wait_bytes(colrecv, col_r)
-        col = colsend[...] + jnp.sum(colrecv[...], axis=0)
-        inverse = 1.0 / jnp.sum(col, axis=0, keepdims=True)
-        icol = jnp.transpose(jnp.broadcast_to(inverse, (LANES, clusters)))
-        colacc[...] = icol
+        colacc[...] = as_column(1.0 / (colsend[...] + jnp.sum(colrecv[...], axis=0)))
 
         def weigh(b, carry):
             for k in range(CAP // LANES):
@@ -262,97 +287,88 @@
                 live = tags[b, 0:1, at] == (core + 1).astype(F32)
                 p = q * jnp.where(live, 1.0 / jnp.where(live, total, 1.0), 0.0)
                 hi = p.astype(BF16)
-                phi[b, :, at] = hi
-                plo[b, :, at] = (p - hi.astype(F32)).astype(BF16)
+                p2[b, 0:clusters, at] = hi
+                p2[b, clusters : 2 * clusters, at] = (p - hi.astype(F32)).astype(BF16)
                 massacc[...] += p
-            x = rows[b]
-            part = jnp.dot(phi[b], x, preferred_element_type=F32)
-            part = part + jnp.dot(plo[b], x, preferred_element_type=F32)
-
-            @pl.when(b == 0)
-            def _():
-                numsend[...] = part
-
-            @pl.when(b > 0)
-            def _():
-                numsend[...] += part
-
+            part = jnp.dot(p2[b], rows[b], preferred_element_type=F32)
+            numsend[...] += part[0:clusters] + part[clusters : 2 * clusters]
             return carry
 
-        lax.fori_loop(0, blocks, weigh, 0)
+        numsend[...] = jnp.zeros_like(numsend)
+        lax.fori_loop(0, blocks, weigh, 0, unroll=True)
         each_peer(rs_copy)
+        masssend[...] = as_row(massacc[...])
         each_peer(mass_copy)
+
+        @pl.when(step == ITERS - 1)
+        def _():
+            def p_start(d, carry):
+                p_copy(d).start()
+                p_forward(d).start()
+                return carry
+
+            lax.fori_loop(0, GROUPS, p_start, 0)
+
         wait_bytes(colrecv, col_s)
         wait_bytes(massrecv, m_r)
+        massacc[...] = as_column(masssend[...] + jnp.sum(massrecv[...], axis=0))
         wait_bytes(numrecv, rs_r)
-        mass = massacc[mine, :] + jnp.sum(massrecv[...], axis=0)
         num = numsend[mine, :] + jnp.sum(numrecv[...], axis=0)
-        call[mine, :] = num / jnp.sum(mass, axis=1, keepdims=True)
+        call[mine, :] = num / massacc[mine, 0:1]
         each_peer(ag_copy)
         wait_bytes(massrecv, m_s)
         wait_bytes(numrecv, rs_s)
         wait_bytes(call.at[rest], ag_r)
-        wait_bytes(call.at[rest], ag_s)
-        split(call[...])
 
         @pl.when(step < ITERS - 1)
         def _():
+            split(call[...])
             colacc[...] = jnp.zeros_like(colacc)
 
             def soft(b, carry):
                 first_soft(b, 0, CAP)
                 return carry
 
-            lax.fori_loop(0, blocks, soft, 0)
-
+            lax.fori_loop(0, blocks, soft, 0, unroll=True)
+
+        wait_bytes(call.at[rest], ag_s)
         return carry
 
     lax.fori_loop(0, ITERS, update, 0)
 
-    pcopy = pltpu.make_async_remote_copy(
-        phi.at[pl.ds(other * GROUPS, GROUPS)], pother, po_s, po_r, device_id=sib, device_id_type=MESH
-    )
-    pcopy.start()
-    ccopy = pltpu.make_async_remote_copy(call, cother, co_s, co_r, device_id=sib, device_id_type=MESH)
+    ccopy = pltpu.make_async_remote_copy(call, cent_out.at[core], co_s, co_r, device_id=sib, device_id_type=MESH)
     ccopy.start()
-    own_out = pltpu.make_async_copy(call, cout_ref.at[core], in_sem.at[0])
+    own_out = pltpu.make_async_copy(call, cent_out.at[core], in_sem.at[0])
     own_out.start()
     wait_bytes(sendbuf, asend)
     wait_bytes(sendtag, tsend)
     wait_bytes(rows.at[pl.ds(0, GROUPS)], fsend)
     wait_bytes(tags.at[pl.ds(0, GROUPS)], ftsend)
-    pcopy.wait()
+
+    def drain(d, carry):
+        rows_copy(d).wait()
+        p_copy(d).wait()
+        p_forward(d).wait()
+        return carry
+
+    lax.fori_loop(0, GROUPS, drain, 0)
     ccopy.wait()
-    other_out = pltpu.make_async_copy(cother, cout_ref.at[other], in_sem.at[1])
-    other_out.start()
-    ohi = cother[...].astype(BF16)
-    olo = (cother[...] - ohi.astype(F32)).astype(BF16)
-    x_ref[0:clusters, :] = ohi
-    x_ref[clusters : 2 * clusters, :] = olo
-
-    def out_copy(d):
-        return pltpu.make_async_copy(res.at[d], rout_ref.at[lax.rem(i + GROUPS - d, GROUPS)], out_sem.at[d])
-
-    def finish(d, carry):
-        p = phi[core * GROUPS + d]
-        recon = lax.dot_general(p, chi[...], TN, preferred_element_type=F32)
-        recon = recon + lax.dot_general(p, clo[...], TN, preferred_element_type=F32)
-        p = pother[d]
-        recon = recon + lax.dot_general(p, x_ref[0:clusters, :], TN, preferred_element_type=F32)
-        recon = recon + lax.dot_general(p, x_ref[clusters : 2 * clusters, :], TN, preferred_element_type=F32)
-        res[d] = rows[core * GROUPS + d].astype(F32) - recon
-        out_copy(d).start()
-        return carry
-
-    lax.fori_loop(0, GROUPS, finish, 0)
     own_out.wait()
-    other_out.wait()
-
-    def drain(d, carry):
-        out_copy(d).wait()
-        return carry
-
-    lax.fori_loop(0, GROUPS, drain, 0)
+
+
+def finish(p_ref, rows_ref, cent_ref, cout_ref, rout_ref, chi, clo):
+    @pl.when(pl.program_id(0) == 0)
+    def _():
+        c = cent_ref[...]
+        hi = c.astype(BF16)
+        chi[...] = hi
+        clo[...] = (c - hi.astype(F32)).astype(BF16)
+        cout_ref[...] = c
+
+    p = p_ref[0]
+    recon = lax.dot_general(p, chi[...], TN, preferred_element_type=F32)
+    recon = recon + lax.dot_general(p, clo[...], TN, preferred_element_type=F32)
+    rout_ref[0] = rows_ref[0].astype(F32) - recon
 
 
 def per_device(residuals, codes, counts, centroids):
@@ -370,47 +386,61 @@
         pltpu.VMEM((blocks, CAP, width), BF16),
         pltpu.VMEM((blocks, 8, CAP), F32),
         pltpu.VMEM((blocks, clusters, CAP), F32),
-        pltpu.VMEM((blocks, clusters, CAP), BF16),
-        pltpu.VMEM((blocks, clusters, CAP), BF16),
-        pltpu.VMEM((8, clusters), F32),
-        pltpu.VMEM((CHIPS - 1, 8, clusters), F32),
+        pltpu.VMEM((blocks, 2 * clusters, CAP), BF16),
+        pltpu.VMEM((1, clusters), F32),
+        pltpu.VMEM((CHIPS - 1, 1, clusters), F32),
         pltpu.VMEM((clusters, width), F32),
         pltpu.VMEM((CHIPS - 1, share, width), F32),
-        pltpu.VMEM((clusters, LANES), F32),
-        pltpu.VMEM((CHIPS - 1, share, LANES), F32),
+        pltpu.VMEM((1, clusters), F32),
+        pltpu.VMEM((CHIPS - 1, 1, clusters), F32),
         pltpu.VMEM((clusters, width), F32),
-        pltpu.VMEM((clusters, width), BF16),
-        pltpu.VMEM((clusters, width), BF16),
+        pltpu.VMEM((2 * clusters, width), BF16),
         pltpu.VMEM((clusters, LANES), F32),
         pltpu.VMEM((clusters, LANES), F32),
-        pltpu.VMEM((GROUPS, clusters, CAP), BF16),
-        pltpu.VMEM((clusters, width), F32),
-        pltpu.VMEM((GROUPS, CAP, width), F32),
+        pltpu.VMEM((clusters, LANES), F32),
         dma((2,)),
         dma, dma, dma((GROUPS - 1, quarters)), dma((GROUPS - 1,)),
         dma, dma, dma((GROUPS, quarters)), dma((GROUPS,)),
         dma, dma, dma, dma, dma, dma, dma, dma,
-        dma, dma, dma, dma, dma((GROUPS,)),
+        dma((GROUPS,)), dma((GROUPS,)), dma, dma,
+        dma((GROUPS,)), dma((GROUPS,)),
     ]
-    cent, resid = pl.pallas_call(
+    hbm = pl.BlockSpec(memory_space=pl.ANY)
+    cent, rows, weights = pl.pallas_call(
         kernel,
         out_shape=(
             jax.ShapeDtypeStruct(centroids.shape, F32),
-            jax.ShapeDtypeStruct((GROUPS, CAP, width), F32),
+            jax.ShapeDtypeStruct((GROUPS, CAP, width), BF16),
+            jax.ShapeDtypeStruct((GROUPS, 2, clusters, CAP), BF16),
         ),
-        in_specs=[
-            pl.BlockSpec(memory_space=pl.ANY),
-            pl.BlockSpec(memory_space=pltpu.VMEM),
-            pl.BlockSpec(memory_space=pltpu.SMEM),
-            pl.BlockSpec(memory_space=pl.ANY),
-        ],
-        out_specs=(pl.BlockSpec(memory_space=pl.ANY), pl.BlockSpec(memory_space=pl.ANY)),
+        in_specs=[hbm, pl.BlockSpec(memory_space=pltpu.VMEM), pl.BlockSpec(memory_space=pltpu.SMEM), hbm],
+        out_specs=(hbm, hbm, hbm),
         scratch_shapes=scratch,
         compiler_params=pltpu.CompilerParams(
             collective_id=0, has_side_effects=True, vmem_limit_bytes=56 * 1024 * 1024
         ),
     )(residuals, codes.reshape(1, nrow), counts.reshape(GROUPS), centroids)
-    return cent, resid.reshape(1, 1, GROUPS * CAP, width)
+    both = 2 * clusters
+    cent, resid = pl.pallas_call(
+        finish,
+        grid=(GROUPS,),
+        out_shape=(
+            jax.ShapeDtypeStruct((both, width), F32),
+            jax.ShapeDtypeStruct((GROUPS, CAP, width), F32),
+        ),
+        in_specs=[
+            pl.BlockSpec((1, both, CAP), lambda s: (s, 0, 0)),
+            pl.BlockSpec((1, CAP, width), lambda s: (s, 0, 0)),
+            pl.BlockSpec((both, width), lambda s: (0, 0)),
+        ],
+        out_specs=(
+            pl.BlockSpec((both, width), lambda s: (0, 0)),
+            pl.BlockSpec((1, CAP, width), lambda s: (s, 0, 0)),
+        ),
+        scratch_shapes=[pltpu.VMEM((both, width), BF16), pltpu.VMEM((both, width), BF16)],
+        compiler_params=pltpu.CompilerParams(vmem_limit_bytes=56 * 1024 * 1024),
+    )(weights.reshape(GROUPS, both, CAP), rows, cent.reshape(both, width))
+    return cent.reshape(2, clusters, width), resid.reshape(1, 1, GROUPS * CAP, width)
 
 
 def solution(mesh):

time: 196 us -> 167 us (0.85)
  Pallas kernels: 186 us -> 166 us
  local copies, waits for them, and re-layouts: 8.54 us -> 0 us
    pallas_call x1, Pallas kernels: 186 us -> 158 us  [per_device(): pl.pallas_call(kernel, out_shape=(jax.ShapeDtypeStruct(centroids.shape, F...]
    unnamed x2 -> x0, local copies, waits for them, and re-layouts: 8.54 us -> none
    pallas_call x0 -> x1, Pallas kernels: none -> 8.29 us  [per_device(): pl.pallas_call(finish, grid=(GROUPS,), out_shape=(jax.ShapeDtypeStruct((b...]
where the time goes in v2:
time: 167 us
  Pallas kernels  166 us (99%)
    pallas_call x1, Pallas kernels, per_device(): pl.pallas_call(kernel, out_shape=(jax.ShapeDtypeStruct(centroids.shape, F...  158 us
    pallas_call x1, Pallas kernels, per_device(): pl.pallas_call(finish, grid=(GROUPS,), out_shape=(jax.ShapeDtypeStruct((b...  8.29 us

profile of v2, /device:TPU:1, one launch (start us, length us, event | category | flops | bytes accessed | tf_op | source)
XLA Modules:
  0.0 167.1 jit_solution(2887732949246036601)
XLA Ops:
  0.6 158.1 %shard_map.59 = (f32[2,256,768]{2,1,0:T(8,128)}, bf16[4,512,768]{2,1,0:T(8,128)(2,1)}, bf16[4,2,256,512]{3,2,1,0:T(8,128)(2,1)}) custom-call(bf16[1024,768]{1,0:T(8,128)(2,1)} %x_hbm.1, s32[1,1024]{1,0:T(1,128)} %bitcast.8, s32[4]{0:T(128)} %bitcast.9, f32[2,256,768]{2,1,0:T(8,128)} %cent_hbm.1), custom_call_target="tpu_custom_call" | custom-call | tf_op jit(solution)/shard_map/pallas_call | solution.py:409
  158.8 8.3 %shard_map.60 = (f32[512,768]{1,0:T(8,128)}, f32[4,512,768]{2,1,0:T(8,128)}) custom-call(bf16[4,512,512]{2,1,0:T(8,128)(2,1)} %bitcast.6, bf16[4,512,768]{2,1,0:T(8,128)(2,1)} %get-tuple-element.8.rows_ref, f32[512,768]{1,0:T(8,128)} %bitcast.7), custom_call_target="tpu_custom_call" | custom-call | tf_op jit(solution)/shard_map/pallas_call | solution.py:424

commit v3 on v2

--- a/solution.py
+++ b/solution.py
@@ -8,6 +8,7 @@
 ITERS = 3
 SCORE_SCALE = 0.0625
 LOG2E = 1.4426950408889634
+FULL = 32767.0
 MESH = pl.DeviceIdType.MESH
 GROUPS = 4
 CHIPS = 16
@@ -15,6 +16,7 @@
 LANES = 128
 CAP = 512
 CHUNK = 128
+TILE = 512
 F32 = jnp.float32
 BF16 = jnp.bfloat16
 
@@ -28,10 +30,10 @@
 
 def kernel(
     x_hbm, codes_ref, counts_ref, cent_hbm, cent_out, rows_out, p_out,
-    x_ref, cent_ref, sendbuf, sendtag, rows, tags, p0, p2, colsend, colrecv, numsend, numrecv,
-    masssend, massrecv, call, c2, cn, colacc, massacc,
+    x_ref, cent_ref, sendbuf, sendtag, rows, tags, p0, p2, colsend, colrecv, numsend, codesend, numrecv,
+    masssend, massrecv, call, callcode, scalesend, scalerecv, c2, cn, colacc, massacc,
     in_sem, asend, tsend, arecv, trecv, fsend, ftsend, frecv, ftrecv,
-    col_s, col_r, rs_s, rs_r, m_s, m_r, ag_s, ag_r, po_s, po_r, co_s, co_r, rows_sem, p_sem,
+    col_s, col_r, rs_s, rs_r, m_s, m_r, ag_s, ag_r, sc_s, sc_r, po_s, po_r, co_s, co_r, rows_sem, p_sem,
 ):
     i = lax.axis_index("code")
     j = lax.axis_index("row")
@@ -150,19 +152,22 @@
         norm = jnp.sum(c * c, axis=1, keepdims=True) * (SCORE_SCALE * LOG2E)
         cn[...] = jnp.broadcast_to(norm, cn.shape)
 
-    def first_soft(b, lo, n):
-        x = rows[b, pl.ds(lo, n), :]
+    def first_soft(parts, n):
+        x = [rows[b, pl.ds(lo, n), :] for b, lo in parts]
+        x = x[0] if len(x) == 1 else jnp.concatenate(x, axis=0)
         s = lax.dot_general(c2[...], x, NT, preferred_element_type=F32)
         s = s[0:clusters] + s[clusters : 2 * clusters]
-        for k in range(n // LANES):
-            at = pl.ds(lo + k * LANES, LANES)
-            t = s[:, k * LANES : (k + 1) * LANES] * (2.0 * SCORE_SCALE * LOG2E) - cn[...]
-            e = jnp.exp2(t - jnp.max(t, axis=0, keepdims=True))
-            total = jnp.sum(e, axis=0, keepdims=True)
-            live = tags[b, 0:1, at] == (core + 1).astype(F32)
-            p = e * jnp.where(live, 1.0 / total, 0.0)
-            p0[b, :, at] = p
-            colacc[...] += p
+        for m, (b, lo) in enumerate(parts):
+            for k in range(n // LANES):
+                at = pl.ds(lo + k * LANES, LANES)
+                first = m * n + k * LANES
+                t = s[:, first : first + LANES] * (2.0 * SCORE_SCALE * LOG2E) - cn[...]
+                e = jnp.exp2(t - jnp.max(t, axis=0, keepdims=True))
+                total = jnp.sum(e, axis=0, keepdims=True)
+                live = tags[b, 0:1, at] == (core + 1).astype(F32)
+                p = e * jnp.where(live, 1.0 / total, 0.0)
+                p0[b, :, at] = p
+                colacc[...] += p
 
     load_c.wait()
     split(cent_ref[...])
@@ -170,6 +175,16 @@
 
     other = 1 - core
 
+    first_soft([(core * GROUPS, 0)], CAP)
+    forward_tag(0).wait_recv()
+
+    def sib_wait(q, carry):
+        forward_copy(0, q).wait_recv()
+        return carry
+
+    lax.fori_loop(0, quarters, sib_wait, 0)
+    first_soft([(other * GROUPS, 0)], CAP)
+
     for d in (2, 1, 3):
         tag_copy(d).wait_recv()
         forward_tag(d).start()
@@ -178,36 +193,19 @@
         forward_tag(d).wait_recv()
         return carry
 
-    lax.fori_loop(0, GROUPS, sib_tag, 0)
-
-    def sib_soft(d, q):
-        forward_copy(d, q).wait_recv()
-        first_soft(other * GROUPS + d, pl.multiple_of(q * CHUNK, CHUNK), CHUNK)
-
-    def own_soft(q, carry):
-        first_soft(core * GROUPS, pl.multiple_of(q * CHUNK, CHUNK), CHUNK)
-        sib_soft(0, q)
-        return carry
-
-    lax.fori_loop(0, quarters, own_soft, 0)
-
-    def place(t):
-        return lax.rem(t, GROUPS - 1) + 1, lax.div(t, GROUPS - 1)
-
-    def arrive(t, carry):
-        d, q = place(t)
-        a2a_copy(d, q).wait_recv()
-        forward_copy(d, q).start()
-        first_soft(core * GROUPS + d, pl.multiple_of(q * CHUNK, CHUNK), CHUNK)
-
-        @pl.when(t > 0)
-        def _():
-            sib_soft(*place(t - 1))
-
-        return carry
-
-    arrivals = quarters * (GROUPS - 1)
-    lax.fori_loop(0, arrivals, arrive, 0)
+    lax.fori_loop(1, GROUPS, sib_tag, 0)
+
+    for q in range(quarters):
+        for d in (1, 3, 2):
+            a2a_copy(d, q).wait_recv()
+            forward_copy(d, q).start()
+        if q == 0:
+            first_soft([(core * GROUPS + d, 0) for d in (1, 3, 2)], CHUNK)
+            continue
+        for d in (1, 3, 2):
+            forward_copy(d, q - 1).wait_recv()
+        for d in (1, 3, 2):
+            first_soft([(core * GROUPS + d, q * CHUNK), (other * GROUPS + d, (q - 1) * CHUNK)], CHUNK)
 
     def rows_copy(d):
         return pltpu.make_async_copy(rows.at[core * GROUPS + d], rows_out.at[source(d)], rows_sem.at[d])
@@ -228,7 +226,9 @@
         return carry
 
     lax.fori_loop(0, GROUPS, rows_start, 0)
-    sib_soft(GROUPS - 1, quarters - 1)
+    for d in (1, 3, 2):
+        forward_copy(d, quarters - 1).wait_recv()
+    first_soft([(other * GROUPS + d, (quarters - 1) * CHUNK) for d in (1, 3, 2)], CHUNK)
 
     def chunk_of(t):
         return pl.ds(pl.multiple_of(t * share, share), share)
@@ -243,7 +243,7 @@
     def rs_copy(d):
         t = chip_at(d)
         return pltpu.make_async_remote_copy(
-            numsend.at[chunk_of(t)], numrecv.at[d - 1], rs_s, rs_r, device_id=row_peer(t), device_id_type=MESH
+            codesend.at[chunk_of(t)], numrecv.at[d - 1], rs_s, rs_r, device_id=row_peer(t), device_id_type=MESH
         )
 
     def mass_copy(d):
@@ -253,8 +253,20 @@
 
     def ag_copy(d):
         return pltpu.make_async_remote_copy(
-            call.at[mine], call.at[mine], ag_s, ag_r, device_id=row_peer(chip_at(d)), device_id_type=MESH
-        )
+            callcode.at[mine], callcode.at[mine], ag_s, ag_r, device_id=row_peer(chip_at(d)), device_id_type=MESH
+        )
+
+    def scale_copy(d):
+        return pltpu.make_async_remote_copy(
+            scalesend, scalerecv.at[d - 1], sc_s, sc_r, device_id=row_peer(chip_at(d)), device_id_type=MESH
+        )
+
+    def encode(v):
+        top = jnp.maximum(jnp.max(jnp.abs(v), axis=1, keepdims=True), 1e-34)
+        return jnp.round(v * (FULL / top)).astype(jnp.int32).astype(jnp.int16), top * (1.0 / FULL)
+
+    def decode(code, scale):
+        return code.astype(jnp.int32).astype(F32) * scale
 
     def each_peer(make):
         def body(d, carry):
@@ -296,9 +308,13 @@
 
         numsend[...] = jnp.zeros_like(numsend)
         lax.fori_loop(0, blocks, weigh, 0, unroll=True)
+        code, scale = encode(numsend[...])
+        codesend[...] = code
         each_peer(rs_copy)
-        masssend[...] = as_row(massacc[...])
+        masssend[0:1, :] = as_row(massacc[...])
+        masssend[1:2, :] = jnp.transpose(jnp.broadcast_to(scale, (clusters, LANES)))[0:1, :]
         each_peer(mass_copy)
+        massrecv[CHIPS - 1] = masssend[...]
 
         @pl.when(step == ITERS - 1)
         def _():
@@ -310,15 +326,29 @@
             lax.fori_loop(0, GROUPS, p_start, 0)
 
         wait_bytes(colrecv, col_s)
-        wait_bytes(massrecv, m_r)
-        massacc[...] = as_column(masssend[...] + jnp.sum(massrecv[...], axis=0))
+        wait_bytes(massrecv.at[pl.ds(0, CHIPS - 1)], m_r)
+        massacc[...] = as_column(jnp.sum(massrecv[:, 0:1, :], axis=0))
+        scales = jnp.concatenate(
+            [massrecv[:, 1, :], jnp.zeros((LANES - CHIPS, clusters), F32)], axis=0
+        )
+        colacc[...] = jnp.transpose(scales)
         wait_bytes(numrecv, rs_r)
-        num = numsend[mine, :] + jnp.sum(numrecv[...], axis=0)
-        call[mine, :] = num / massacc[mine, 0:1]
+        num = numsend[mine, :]
+        for d in range(CHIPS - 1):
+            num = num + decode(numrecv[d], colacc[mine, d : d + 1])
+        code, scale = encode(num / massacc[mine, 0:1])
+        callcode[mine, :] = code
         each_peer(ag_copy)
-        wait_bytes(massrecv, m_s)
+        massacc[...] = jnp.zeros_like(massacc)
+        massacc[mine, :] = jnp.broadcast_to(scale, (share, LANES))
+        scalesend[...] = jnp.transpose(massacc[...])[0:1, :]
+        each_peer(scale_copy)
+        wait_bytes(massrecv.at[pl.ds(0, CHIPS - 1)], m_s)
         wait_bytes(numrecv, rs_s)
-        wait_bytes(call.at[rest], ag_r)
+        wait_bytes(scalerecv, sc_r)
+        colacc[...] = as_column(scalesend[...] + jnp.sum(scalerecv[...], axis=0))
+        wait_bytes(callcode.at[rest], ag_r)
+        call[...] = decode(callcode[...], colacc[:, 0:1])
 
         @pl.when(step < ITERS - 1)
         def _():
@@ -326,12 +356,13 @@
             colacc[...] = jnp.zeros_like(colacc)
 
             def soft(b, carry):
-                first_soft(b, 0, CAP)
+                first_soft([(b, 0)], CAP)
                 return carry
 
             lax.fori_loop(0, blocks, soft, 0, unroll=True)
 
-        wait_bytes(call.at[rest], ag_s)
+        wait_bytes(callcode.at[rest], ag_s)
+        wait_bytes(scalerecv, sc_s)
         return carry
 
     lax.fori_loop(0, ITERS, update, 0)
@@ -357,7 +388,7 @@
 
 
 def finish(p_ref, rows_ref, cent_ref, cout_ref, rout_ref, chi, clo):
-    @pl.when(pl.program_id(0) == 0)
+    @pl.when((pl.program_id(0) == 0) & (pl.program_id(1) == 0))
     def _():
         c = cent_ref[...]
         hi = c.astype(BF16)
@@ -390,10 +421,14 @@
         pltpu.VMEM((1, clusters), F32),
         pltpu.VMEM((CHIPS - 1, 1, clusters), F32),
         pltpu.VMEM((clusters, width), F32),
-        pltpu.VMEM((CHIPS - 1, share, width), F32),
+        pltpu.VMEM((clusters, width), jnp.int16),
+        pltpu.VMEM((CHIPS - 1, share, width), jnp.int16),
+        pltpu.VMEM((2, clusters), F32),
+        pltpu.VMEM((CHIPS, 2, clusters), F32),
+        pltpu.VMEM((clusters, width), F32),
+        pltpu.VMEM((clusters, width), jnp.int16),
         pltpu.VMEM((1, clusters), F32),
         pltpu.VMEM((CHIPS - 1, 1, clusters), F32),
-        pltpu.VMEM((clusters, width), F32),
         pltpu.VMEM((2 * clusters, width), BF16),
         pltpu.VMEM((clusters, LANES), F32),
         pltpu.VMEM((clusters, LANES), F32),
@@ -401,7 +436,7 @@
         dma((2,)),
         dma, dma, dma((GROUPS - 1, quarters)), dma((GROUPS - 1,)),
         dma, dma, dma((GROUPS, quarters)), dma((GROUPS,)),
-        dma, dma, dma, dma, dma, dma, dma, dma,
+        dma, dma, dma, dma, dma, dma, dma, dma, dma, dma,
         dma((GROUPS,)), dma((GROUPS,)), dma, dma,
         dma((GROUPS,)), dma((GROUPS,)),
     ]
@@ -423,19 +458,19 @@
     both = 2 * clusters
     cent, resid = pl.pallas_call(
         finish,
-        grid=(GROUPS,),
+        grid=(GROUPS, CAP // TILE),
         out_shape=(
             jax.ShapeDtypeStruct((both, width), F32),
             jax.ShapeDtypeStruct((GROUPS, CAP, width), F32),
         ),
         in_specs=[
-            pl.BlockSpec((1, both, CAP), lambda s: (s, 0, 0)),
-            pl.BlockSpec((1, CAP, width), lambda s: (s, 0, 0)),
-            pl.BlockSpec((both, width), lambda s: (0, 0)),
+            pl.BlockSpec((1, both, TILE), lambda s, t: (s, 0, t)),
+            pl.BlockSpec((1, TILE, width), lambda s, t: (s, t, 0)),
+            pl.BlockSpec((both, width), lambda s, t: (0, 0)),
         ],
         out_specs=(
-            pl.BlockSpec((both, width), lambda s: (0, 0)),
-            pl.BlockSpec((1, CAP, width), lambda s: (s, 0, 0)),
+            pl.BlockSpec((both, width), lambda s, t: (0, 0)),
+            pl.BlockSpec((1, TILE, width), lambda s, t: (s, t, 0)),
         ),
         scratch_shapes=[pltpu.VMEM((both, width), BF16), pltpu.VMEM((both, width), BF16)],
         compiler_params=pltpu.CompilerParams(vmem_limit_bytes=56 * 1024 * 1024),

time: 167 us -> 142 us (0.85)
  Pallas kernels: 166 us -> 142 us
    pallas_call x1, Pallas kernels: 158 us -> 133 us  [per_device(): pl.pallas_call(kernel, out_shape=(jax.ShapeDtypeStruct(centroids.shape, F...]
where the time goes in v3:
time: 142 us
  Pallas kernels  142 us (100%)
    pallas_call x1, Pallas kernels, per_device(): pl.pallas_call(kernel, out_shape=(jax.ShapeDtypeStruct(centroids.shape, F...  133 us
    pallas_call x1, Pallas kernels, per_device(): pl.pallas_call(finish, grid=(GROUPS, CAP // TILE), out_shape=(jax.ShapeDt...  8.3 us

profile of v3, /device:TPU:1, one launch (start us, length us, event | category | flops | bytes accessed | tf_op | source)
XLA Modules:
  0.0 142.2 jit_solution(2013680624488193810)
XLA Ops:
  0.6 133.3 %shard_map.59 = (f32[2,256,768]{2,1,0:T(8,128)}, bf16[4,512,768]{2,1,0:T(8,128)(2,1)}, bf16[4,2,256,512]{3,2,1,0:T(8,128)(2,1)}) custom-call(bf16[1024,768]{1,0:T(8,128)(2,1)} %x_hbm.1, s32[1,1024]{1,0:T(1,128)} %bitcast.8, s32[4]{0:T(128)} %bitcast.9, f32[2,256,768]{2,1,0:T(8,128)} %cent_hbm.1), custom_call_target="tpu_custom_call" | custom-call | tf_op jit(solution)/shard_map/pallas_call | solution.py:444
  133.9 8.3 %shard_map.60 = (f32[512,768]{1,0:T(8,128)}, f32[4,512,768]{2,1,0:T(8,128)}) custom-call(bf16[4,512,512]{2,1,0:T(8,128)(2,1)} %bitcast.6, bf16[4,512,768]{2,1,0:T(8,128)(2,1)} %get-tuple-element.8.rows_ref, f32[512,768]{1,0:T(8,128)} %bitcast.7), custom_call_target="tpu_custom_call" | custom-call | tf_op jit(solution)/shard_map/pallas_call | solution.py:459

commit v4 on v3

--- a/solution.py
+++ b/solution.py
@@ -13,10 +13,13 @@
 GROUPS = 4
 CHIPS = 16
 SIDE = 4
+FAR_FIRST = sorted(
+    [(z, x) for z in range(SIDE) for x in range(SIDE) if z or x],
+    key=lambda s: -min(s[0], SIDE - s[0]) - min(s[1], SIDE - s[1]),
+)
 LANES = 128
 CAP = 512
 CHUNK = 128
-TILE = 512
 F32 = jnp.float32
 BF16 = jnp.bfloat16
 
@@ -46,8 +49,10 @@
     clusters = call.shape[0]
     width = call.shape[1]
 
+    peers = [lax.rem(cz + dz, SIDE) * SIDE + lax.rem(cx + dx, SIDE) for dz, dx in FAR_FIRST]
+
     def chip_at(d):
-        return lax.rem(cz + lax.div(d, SIDE), SIDE) * SIDE + lax.rem(cx + lax.rem(d, SIDE), SIDE)
+        return peers[d - 1]
 
     def row_peer(t):
         return (i, 2 * t + core)
@@ -68,11 +73,8 @@
         pl.semaphore_signal(barrier, inc=1, device_id=(group(d), j), device_id_type=MESH)
     pl.semaphore_signal(barrier, inc=1, device_id=sib, device_id_type=MESH)
 
-    def greet(d, carry):
+    for d in range(1, CHIPS):
         pl.semaphore_signal(barrier, inc=1, device_id=row_peer(chip_at(d)), device_id_type=MESH)
-        return carry
-
-    lax.fori_loop(1, CHIPS, greet, 0)
 
     load_x.wait()
     half = CAP // 2
@@ -269,11 +271,8 @@
         return code.astype(jnp.int32).astype(F32) * scale
 
     def each_peer(make):
-        def body(d, carry):
+        for d in range(1, CHIPS):
             make(d).start()
-            return carry
-
-        lax.fori_loop(1, CHIPS, body, 0)
 
     blocks = 2 * GROUPS
     rest = pl.ds(0, (CHIPS - 1) * share)
@@ -387,19 +386,24 @@
     own_out.wait()
 
 
-def finish(p_ref, rows_ref, cent_ref, cout_ref, rout_ref, chi, clo):
-    @pl.when((pl.program_id(0) == 0) & (pl.program_id(1) == 0))
-    def _():
-        c = cent_ref[...]
-        hi = c.astype(BF16)
-        chi[...] = hi
-        clo[...] = (c - hi.astype(F32)).astype(BF16)
-        cout_ref[...] = c
-
-    p = p_ref[0]
-    recon = lax.dot_general(p, chi[...], TN, preferred_element_type=F32)
-    recon = recon + lax.dot_general(p, clo[...], TN, preferred_element_type=F32)
-    rout_ref[0] = rows_ref[0].astype(F32) - recon
+def finish(p_ref, rows_ref, cent_ref, cout_ref, rout_ref, chi, clo, res, cent_sem, sem):
+    cent_copy = pltpu.make_async_copy(cent_ref, cout_ref, cent_sem)
+    cent_copy.start()
+    c = cent_ref[...].reshape(chi.shape)
+    hi = c.astype(BF16)
+    chi[...] = hi
+    clo[...] = (c - hi.astype(F32)).astype(BF16)
+    copies = []
+    for s in range(GROUPS):
+        p = p_ref[s].reshape(chi.shape[0], CAP)
+        recon = lax.dot_general(p, chi[...], TN, preferred_element_type=F32)
+        recon = recon + lax.dot_general(p, clo[...], TN, preferred_element_type=F32)
+        res[s] = rows_ref[s].astype(F32) - recon
+        copies.append(pltpu.make_async_copy(res.at[s], rout_ref.at[s], sem.at[s]))
+        copies[-1].start()
+    for copy in copies:
+        copy.wait()
+    cent_copy.wait()
 
 
 def per_device(residuals, codes, counts, centroids):
@@ -441,15 +445,16 @@
         dma((GROUPS,)), dma((GROUPS,)),
     ]
     hbm = pl.BlockSpec(memory_space=pl.ANY)
+    vmem = pl.BlockSpec(memory_space=pltpu.VMEM)
     cent, rows, weights = pl.pallas_call(
         kernel,
         out_shape=(
-            jax.ShapeDtypeStruct(centroids.shape, F32),
-            jax.ShapeDtypeStruct((GROUPS, CAP, width), BF16),
-            jax.ShapeDtypeStruct((GROUPS, 2, clusters, CAP), BF16),
+            pltpu.VMEM(centroids.shape, F32),
+            pltpu.VMEM((GROUPS, CAP, width), BF16),
+            pltpu.VMEM((GROUPS, 2, clusters, CAP), BF16),
         ),
-        in_specs=[hbm, pl.BlockSpec(memory_space=pltpu.VMEM), pl.BlockSpec(memory_space=pltpu.SMEM), hbm],
-        out_specs=(hbm, hbm, hbm),
+        in_specs=[hbm, vmem, pl.BlockSpec(memory_space=pltpu.SMEM), hbm],
+        out_specs=(vmem, vmem, vmem),
         scratch_shapes=scratch,
         compiler_params=pltpu.CompilerParams(
             collective_id=0, has_side_effects=True, vmem_limit_bytes=56 * 1024 * 1024
@@ -458,24 +463,22 @@
     both = 2 * clusters
     cent, resid = pl.pallas_call(
         finish,
-        grid=(GROUPS, CAP // TILE),
         out_shape=(
-            jax.ShapeDtypeStruct((both, width), F32),
+            jax.ShapeDtypeStruct(centroids.shape, F32),
             jax.ShapeDtypeStruct((GROUPS, CAP, width), F32),
         ),
-        in_specs=[
-            pl.BlockSpec((1, both, TILE), lambda s, t: (s, 0, t)),
-            pl.BlockSpec((1, TILE, width), lambda s, t: (s, t, 0)),
-            pl.BlockSpec((both, width), lambda s, t: (0, 0)),
+        in_specs=[vmem, vmem, vmem],
+        out_specs=(hbm, hbm),
+        scratch_shapes=[
+            pltpu.VMEM((both, width), BF16),
+            pltpu.VMEM((both, width), BF16),
+            pltpu.VMEM((GROUPS, CAP, width), F32),
+            dma,
+            dma((GROUPS,)),
         ],
-        out_specs=(
-            pl.BlockSpec((both, width), lambda s, t: (0, 0)),
-            pl.BlockSpec((1, TILE, width), lambda s, t: (s, t, 0)),
-        ),
-        scratch_shapes=[pltpu.VMEM((both, width), BF16), pltpu.VMEM((both, width), BF16)],
-        compiler_params=pltpu.CompilerParams(vmem_limit_bytes=56 * 1024 * 1024),
-    )(weights.reshape(GROUPS, both, CAP), rows, cent.reshape(both, width))
-    return cent.reshape(2, clusters, width), resid.reshape(1, 1, GROUPS * CAP, width)
+        compiler_params=pltpu.CompilerParams(vmem_limit_bytes=20 * 1024 * 1024),
+    )(weights, rows, cent)
+    return cent, resid.reshape(1, 1, GROUPS * CAP, width)
 
 
 def solution(mesh):

time: 142 us -> 137 us (0.965)
  Pallas kernels: 142 us -> 136 us
    pallas_call x2, Pallas kernels: 142 us -> 136 us  [the longest x1 131 us: per_device(): pl.pallas_call(kernel, out_shape=(pltpu.VMEM(centroids.shape, F32), pltpu...]
where the time goes in v4:
time: 137 us; the launch traced here: 136 us
  Pallas kernels  136 us (99%)
    pallas_call x1, Pallas kernels, per_device(): pl.pallas_call(kernel, out_shape=(pltpu.VMEM(centroids.shape, F32), pltpu...  131 us
    pallas_call x1, Pallas kernels, per_device(): pl.pallas_call(finish, out_shape=(jax.ShapeDtypeStruct(centroids.shape, F...  4.66 us

profile of v4, /device:TPU:1, one launch (start us, length us, event | category | flops | bytes accessed | tf_op | source)
XLA Modules:
  0.0 136.3 jit_solution(13354817049654895651)
XLA Ops:
  0.6 130.9 %shard_map.59 = (f32[2,256,768]{2,1,0:T(8,128)S(1)}, bf16[4,512,768]{2,1,0:T(8,128)(2,1)S(1)}, bf16[4,2,256,512]{3,2,1,0:T(8,128)(2,1)S(1)}) custom-call(bf16[1024,768]{1,0:T(8,128)(2,1)} %x_hbm.1, s32[1,1024]{1,0:T(1,128)} %bitcast.3, s32[4]{0:T(128)} %bitcast.4, f32[2,256,768]{2,1,0:T(8,128)} %cent_hbm.1), custom_call_target="tpu_custom_call" | custom-call | tf_op jit(solution)/shard_map/pallas_call | solution.py:449
  131.5 4.7 %shard_map.60 = (f32[2,256,768]{2,1,0:T(8,128)}, f32[4,512,768]{2,1,0:T(8,128)}) custom-call(bf16[4,2,256,512]{3,2,1,0:T(8,128)(2,1)S(1)} %get-tuple-element.7.p_ref, bf16[4,512,768]{2,1,0:T(8,128)(2,1)S(1)} %get-tuple-element.8.rows_ref, f32[2,256,768]{2,1,0:T(8,128)S(1)} %get-tuple-element.9.cent_ref), custom_call_target="tpu_custom_call" | custom-call | tf_op jit(solution)/shard_map/pallas_call | solution.py:464

commit v5 on v4

--- a/solution.py
+++ b/solution.py
@@ -309,10 +309,10 @@
         lax.fori_loop(0, blocks, weigh, 0, unroll=True)
         code, scale = encode(numsend[...])
         codesend[...] = code
-        each_peer(rs_copy)
         masssend[0:1, :] = as_row(massacc[...])
         masssend[1:2, :] = jnp.transpose(jnp.broadcast_to(scale, (clusters, LANES)))[0:1, :]
         each_peer(mass_copy)
+        each_peer(rs_copy)
         massrecv[CHIPS - 1] = masssend[...]
 
         @pl.when(step == ITERS - 1)

time: 137 us -> 138 us (level)
  no operation moved by 1% of the time
where the time goes in v5:
time: 138 us
  Pallas kernels  137 us (99%)
    pallas_call x1, Pallas kernels, per_device(): pl.pallas_call(kernel, out_shape=(pltpu.VMEM(centroids.shape, F32), pltpu...  132 us
    pallas_call x1, Pallas kernels, per_device(): pl.pallas_call(finish, out_shape=(jax.ShapeDtypeStruct(centroids.shape, F...  4.66 us

profile of v5, /device:TPU:1, one launch (start us, length us, event | category | flops | bytes accessed | tf_op | source)
XLA Modules:
  0.0 137.5 jit_solution(9128131586976813011)
XLA Ops:
  0.6 132.0 %shard_map.59 = (f32[2,256,768]{2,1,0:T(8,128)S(1)}, bf16[4,512,768]{2,1,0:T(8,128)(2,1)S(1)}, bf16[4,2,256,512]{3,2,1,0:T(8,128)(2,1)S(1)}) custom-call(bf16[1024,768]{1,0:T(8,128)(2,1)} %x_hbm.1, s32[1,1024]{1,0:T(1,128)} %bitcast.3, s32[4]{0:T(128)} %bitcast.4, f32[2,256,768]{2,1,0:T(8,128)} %cent_hbm.1), custom_call_target="tpu_custom_call" | custom-call | tf_op jit(solution)/shard_map/pallas_call | solution.py:449
  132.7 4.7 %shard_map.60 = (f32[2,256,768]{2,1,0:T(8,128)}, f32[4,512,768]{2,1,0:T(8,128)}) custom-call(bf16[4,2,256,512]{3,2,1,0:T(8,128)(2,1)S(1)} %get-tuple-element.7.p_ref, bf16[4,512,768]{2,1,0:T(8,128)(2,1)S(1)} %get-tuple-element.8.rows_ref, f32[2,256,768]{2,1,0:T(8,128)S(1)} %get-tuple-element.9.cent_ref), custom_call_target="tpu_custom_call" | custom-call | tf_op jit(solution)/shard_map/pallas_call | solution.py:464
